TPU v7x, 32 devices: a whole 2x2x4 slice. The times are simulated.
32 devices in a mesh: node: 16 (over z, x, core), ctrl: 2 (over y).
Axes of the slice: x: 2, y: 2, z: 4, core: 2. Of those that a mesh axis runs over, the one named last changes fastest.
Arguments:
- sensitivity: bfloat16 [96, 65536], P(None, 'node'), may hold values from -1.5 to 1.5
- node_xyz: float32 [3, 65536], P(None, 'node'), may hold values from 0 to 1
- ctrl_xyz: float32 [3, 16384], P(None, 'ctrl'), may hold values from 0 to 1
- inverse: bfloat16 [16384, 16384], P('ctrl', 'node'), may hold values from -0.046875 to 0.046875
Outputs:
- control_grad: float32 [96, 16384], P(None, ('node', 'ctrl'))
All inputs are finite; a program needn't handle non-finite values.
Results may differ from a plain program's by a relative error of at most 0.004.
Values may be sent and summed in bfloat16 or wider, within the bound.
A program may use at most 64 MiB of HBM per device.

v0:
```python
import jax
import jax.numpy as jnp
from jax import lax
from jax.sharding import PartitionSpec as P

support_radius = 0.12


def kernel_tile(node_part, ctrl_xyz):
    delta_x = node_part[0][:, None] - ctrl_xyz[0][None, :]
    delta_y = node_part[1][:, None] - ctrl_xyz[1][None, :]
    delta_z = node_part[2][:, None] - ctrl_xyz[2][None, :]
    scaled = jnp.sqrt(delta_x * delta_x + delta_y * delta_y + delta_z * delta_z) / support_radius
    remain = jnp.maximum(1.0 - scaled, 0.0)
    return (remain**4 * (4.0 * scaled + 1.0)).astype(jnp.bfloat16)


def per_device(sensitivity, node_xyz, ctrl_xyz, inverse):
    nodes_here = node_xyz.shape[1]
    span_rows = min(1024, nodes_here)
    steps_count = nodes_here // span_rows

    def advance(number, running):
        offset = number * span_rows
        node_part = lax.dynamic_slice_in_dim(node_xyz, offset, span_rows, 1)
        sens_part = lax.dynamic_slice_in_dim(sensitivity, offset, span_rows, 1)
        weights_tile = kernel_tile(node_part, ctrl_xyz)
        return running + jnp.dot(sens_part, weights_tile, preferred_element_type=jnp.float32)

    start_sum = jnp.zeros((sensitivity.shape[0], ctrl_xyz.shape[1]), jnp.float32)
    partial_pull = lax.fori_loop(0, steps_count, advance, start_sum)
    pulled_low = lax.psum(partial_pull, "node").astype(jnp.bfloat16)
    product = jnp.dot(pulled_low, inverse, preferred_element_type=jnp.float32)
    return lax.psum_scatter(product, "ctrl", scatter_dimension=1, tiled=True)


def solution(mesh):
    in_specs = (P(None, "node"), P(None, "node"), P(None, "ctrl"), P("ctrl", "node"))
    out_specs = P(None, ("node", "ctrl"))
    return jax.shard_map(
        per_device, mesh=mesh, in_specs=in_specs, out_specs=out_specs, check_vma=False
    )
```

profile of v0, /device:TPU:0, one launch (start us, length us, event | category | flops | bytes accessed | tf_op | source)
XLA Modules:
  0.0 234.7 jit_solution(1626822135103082556)
XLA Ops:
  6.5 0.0 reduce-scatter.2.cloned.1.call-start
  6.5 118.4 %while.16 = (s32[]{:T(128)}, f32[96,8192]{1,0:T(8,128)S(1)}, bf16[96,4096]{1,0:T(8,128)(2,1)}, f32[3,4096]{1,0:T(4,128)}, f32[3,8192]{1,0:T(4,128)}, /*index=5*/...) while((s32[]{:T(128)}, f32[96,8192]{1,0:T(8,128)S(1)}, ...), condition=%wide.region_1.0_spmd.clone, body=%wide.region_0.0_spmd.clone.sunk | while | flops 1754791936 | bytes 6820053 | solution.py:31
  6.5 0.9 constant_dynamic-slice_fusion.2
  7.4 1.2 fusion.18
  8.6 27.5 %fusion.19 = f32[96,8192]{1,0:T(8,128)S(1)} fusion(f32[8192]{0:T(1024)S(1)} %bitcast.21, f32[1024]{0:T(1024)S(1)} %bitcast.25, f32[8192]{0:T(1024)S(1)} %bitcast.22, f32[1024]{0:T(1024)S(1)} %bitcast.24, f32[8192]{0:T(1024)S(1)} %bitcast.20, f32[1024]{0:T(1024)S(1)} %bitcast.23, f32[96,8192]{1,0:T(8,128)S(1)} %get-tuple-element.227, ...), kind=kOutput, calls=%fused_computation.2.clone.1 | convolution fusion | flops 1754791936 | bytes 6598661 | tf_op jit(solution)/shard_map/while/body/eval_jaxpr/dot_general | solution.py:28
  36.1 0.9 constant_dynamic-slice_fusion.2
  37.0 1.2 fusion.18
  38.2 27.4 %fusion.19 = f32[96,8192]{1,0:T(8,128)S(1)} fusion(f32[8192]{0:T(1024)S(1)} %bitcast.21, f32[1024]{0:T(1024)S(1)} %bitcast.25, f32[8192]{0:T(1024)S(1)} %bitcast.22, f32[1024]{0:T(1024)S(1)} %bitcast.24, f32[8192]{0:T(1024)S(1)} %bitcast.20, f32[1024]{0:T(1024)S(1)} %bitcast.23, f32[96,8192]{1,0:T(8,128)S(1)} %get-tuple-element.227, ...), kind=kOutput, calls=%fused_computation.2.clone.1 | convolution fusion | flops 1754791936 | bytes 6598661 | tf_op jit(solution)/shard_map/while/body/eval_jaxpr/dot_general | solution.py:28
  65.7 0.9 constant_dynamic-slice_fusion.2
  66.6 1.2 fusion.18
  67.8 27.4 %fusion.19 = f32[96,8192]{1,0:T(8,128)S(1)} fusion(f32[8192]{0:T(1024)S(1)} %bitcast.21, f32[1024]{0:T(1024)S(1)} %bitcast.25, f32[8192]{0:T(1024)S(1)} %bitcast.22, f32[1024]{0:T(1024)S(1)} %bitcast.24, f32[8192]{0:T(1024)S(1)} %bitcast.20, f32[1024]{0:T(1024)S(1)} %bitcast.23, f32[96,8192]{1,0:T(8,128)S(1)} %get-tuple-element.227, ...), kind=kOutput, calls=%fused_computation.2.clone.1 | convolution fusion | flops 1754791936 | bytes 6598661 | tf_op jit(solution)/shard_map/while/body/eval_jaxpr/dot_general | solution.py:28
  95.3 0.9 constant_dynamic-slice_fusion.2
  96.2 1.2 fusion.18
  97.3 27.4 %fusion.19 = f32[96,8192]{1,0:T(8,128)S(1)} fusion(f32[8192]{0:T(1024)S(1)} %bitcast.21, f32[1024]{0:T(1024)S(1)} %bitcast.25, f32[8192]{0:T(1024)S(1)} %bitcast.22, f32[1024]{0:T(1024)S(1)} %bitcast.24, f32[8192]{0:T(1024)S(1)} %bitcast.20, f32[1024]{0:T(1024)S(1)} %bitcast.23, f32[96,8192]{1,0:T(8,128)S(1)} %get-tuple-element.227, ...), kind=kOutput, calls=%fused_computation.2.clone.1 | convolution fusion | flops 1754791936 | bytes 6598661 | tf_op jit(solution)/shard_map/while/body/eval_jaxpr/dot_general | solution.py:28
  125.0 0.0 copy-start
  125.0 1.6 copy-done
  126.7 79.2 %all-reduce.1 = bf16[96,8192]{1,0:T(8,128)(2,1)S(1)} all-reduce(f32[96,8192]{1,0:T(8,128)} %copy-done), channel_id=1, replica_groups=mesh['node'=16,'ctrl'=2] {'node'}, use_global_device_ids=true, to_apply=%region_2.0 | all-reduce | flops 786432 | bytes 4718592 | tf_op jit(solution)/shard_map/psum | solution.py:32
  205.8 9.3 %fusion.11 = f32[96,1024]{1,0:T(8,128)} fusion(bf16[96,8192]{1,0:T(8,128)(2,1)S(1)} %all-reduce.1, bf16[8192,1024]{1,0:T(8,128)(2,1)} %param.9), kind=kOutput, calls=%fused_computation.13 | convolution fusion | flops 1610612736 | bytes 18743296 | tf_op jit(solution)/shard_map/dot_general | solution.py:33
  215.1 0.0 reduce-scatter.2.cloned.1.call-update
  215.1 12.7 %reduce-scatter.2.cloned.1.call-done = f32[96,512]{1,0:T(8,128)} async-done(((f32[96,1024]{1,0:T(8,128)}), f32[96,512]{1,0:T(8,128)}) %reduce-scatter.2.cloned.1.call-update) | async-done | bytes 196624 | tf_op jit(solution)/shard_map/reduce_scatter | solution.py:34
  (1 shorter events, 0.0 us)
Async XLA Ops:
  6.5 221.3 %reduce-scatter.2.cloned.1.call-start = ((), (), s32[]{:S(2)}) async-start(), calls=%async_computation.1 | async-start | bytes 589824 | tf_op jit(solution)/shard_map/reduce_scatter | solution.py:34
  125.0 1.7 copy-start
Sparse Core Ops, SparseCore 0:
  215.2 12.5 reduce-scatter.1
where the time goes:
time: 235 us
  matrix products  119 us (51%)
  blocking collectives  79.2 us (34%)
  between operations  13.4 us (6%)
  waiting for transfers between devices  12.7 us (5%)
  local copies, waits for them, and re-layouts  10 us (4%)
    dot_general x4, matrix products, advance(): jnp.dot(sens_part, weights_tile, preferred_element_type=jnp.float32)  110 us
    psum x1, blocking collectives, per_device(): pulled_low = lax.psum(partial_pull, 'node').astype(jnp.bfloat16)  79.2 us
    reduce_scatter x1, waiting for transfers between devices, per_device(): return lax.psum_scatter(product, 'ctrl', scatter_dimension=1, tiled=True)  12.7 us
    dot_general x1, matrix products, per_device(): product = jnp.dot(pulled_low, inverse, preferred_element_type=jnp.float32)  9.28 us
    slice x8, local copies, waits for them, and re-layouts, kernel_tile(): delta_x = node_part[0][:, None] - ctrl_xyz[0][None, :]  8.35 us
  transfers between devices with their start and end apart: 1, of which 1 were waited for; matrix products, arithmetic and copies ran while one was open for 0% of the time, Pallas kernels for 0%

commit v1 on v0

v1 whole, which is shorter than its diff:
```python
import functools

import jax
import jax.numpy as jnp
from jax import lax
from jax.experimental import pallas as pl
from jax.experimental.pallas import tpu as pltpu
from jax.sharding import PartitionSpec as P

support_radius = 0.12
feature_rows = 32


def split_three(value):
    high = value.astype(jnp.bfloat16).astype(jnp.float32)
    rest = value - high
    middle = rest.astype(jnp.bfloat16).astype(jnp.float32)
    return high, middle, rest - middle


def feature_pair(xyz, is_node):
    ones = jnp.ones_like(xyz[0:1])
    rows = []
    scaled = (xyz - 0.5) * (4.0 / support_radius)
    for axis in range(3):
        high, middle, low = split_three(scaled[axis : axis + 1])
        if is_node:
            rows += [high, high, middle, middle, high, low]
        else:
            rows += [-2.0 * part for part in (high, middle, high, middle, low, high)]
    square = scaled * scaled
    total = square[0:1] + square[1:2] + square[2:3]
    parts = list(split_three(total))
    rows += parts + [ones] * 3 if is_node else [ones] * 3 + parts
    rows += [jnp.zeros_like(ones)] * (feature_rows - len(rows))
    return rows


def fill_features(wide_ref, xyz_ref, is_node):
    for index, row in enumerate(feature_pair(xyz_ref[...], is_node)):
        wide_ref[pl.ds(index, 1), :] = row


def weights_of(square):
    square = jnp.maximum(square, 1e-12)
    remain = jnp.maximum(4.0 - square * lax.rsqrt(square), 0.0)
    twice = remain * remain
    return ((twice * twice) * (5.0 - remain)).astype(jnp.bfloat16)


def pull_kernel(rows, span, block, sens_ref, node_ref, ctrl_ref, out_ref, node_wide, ctrl_wide, node_feat, ctrl_feat, sens_t):
    nodes, ctrls = node_ref.shape[1], ctrl_ref.shape[1]
    fill_features(node_wide, node_ref, True)
    fill_features(ctrl_wide, ctrl_ref, False)
    node_feat[...] = node_wide[...].astype(jnp.bfloat16)

    @pl.loop(0, nodes // block)
    def _(step):
        here = pl.ds(pl.multiple_of(step * block, block), block)
        sens_t[here, :] = sens_ref[:, here].astype(jnp.float32).T.astype(jnp.bfloat16)

    @pl.loop(0, ctrls // block)
    def _(step):
        here = pl.ds(pl.multiple_of(step * block, block), block)
        ctrl_feat[here, :] = ctrl_wide[:, here].T.astype(jnp.bfloat16)

    @pl.loop(0, ctrls // rows)
    def _(step):
        here = pl.ds(pl.multiple_of(step * rows, rows), rows)
        left = ctrl_feat[here, :]

        def advance(number, total):
            for part in range(span // block):
                offset = pl.multiple_of(number * span + part * block, block)
                square = jnp.dot(left, node_feat[:, pl.ds(offset, block)], preferred_element_type=jnp.float32)
                total = total + jnp.dot(weights_of(square), sens_t[pl.ds(offset, block), :], preferred_element_type=jnp.float32)
            return total

        total = lax.fori_loop(0, nodes // span, advance, jnp.zeros((rows, sens_t.shape[1]), jnp.float32))
        out_ref[:, here] = (total * (1.0 / 256.0)).T


def pull_part(sensitivity, node_xyz, ctrl_xyz):
    objs, nodes = sensitivity.shape
    ctrls = ctrl_xyz.shape[1]
    rows, span, block = min(512, ctrls), min(2048, nodes), min(256, nodes)
    return pl.pallas_call(
        functools.partial(pull_kernel, rows, span, block),
        out_shape=jax.ShapeDtypeStruct((objs, ctrls), jnp.float32),
        in_specs=[pl.BlockSpec(memory_space=pltpu.VMEM)] * 3,
        out_specs=pl.BlockSpec(memory_space=pltpu.VMEM),
        scratch_shapes=[
            pltpu.VMEM((feature_rows, nodes), jnp.float32),
            pltpu.VMEM((feature_rows, ctrls), jnp.float32),
            pltpu.VMEM((feature_rows, nodes), jnp.bfloat16),
            pltpu.VMEM((ctrls, feature_rows), jnp.bfloat16),
            pltpu.VMEM((nodes, objs), jnp.bfloat16),
        ],
        compiler_params=pltpu.CompilerParams(vmem_limit_bytes=48 * 2**20),
    )(sensitivity, node_xyz, ctrl_xyz)


def per_device(sensitivity, node_xyz, ctrl_xyz, inverse):
    partial_pull = pull_part(sensitivity, node_xyz, ctrl_xyz)
    pulled = lax.psum_scatter(partial_pull, "node", scatter_dimension=1, tiled=True)
    pulled_low = lax.all_gather(pulled.astype(jnp.bfloat16), "node", axis=1, tiled=True)
    product = jnp.dot(pulled_low, inverse, preferred_element_type=jnp.float32)
    return lax.psum_scatter(product, "ctrl", scatter_dimension=1, tiled=True)


def solution(mesh):
    in_specs = (P(None, "node"), P(None, "node"), P(None, "ctrl"), P("ctrl", "node"))
    out_specs = P(None, ("node", "ctrl"))
    return jax.shard_map(
        per_device, mesh=mesh, in_specs=in_specs, out_specs=out_specs, check_vma=False
    )
```

time: 235 us -> 211 us (0.90)
  matrix products: 119 us -> 9.79 us
  waiting for transfers between devices: 12.7 us -> 120 us
  blocking collectives: 79.2 us -> 0 us
  Pallas kernels: 0 us -> 63.4 us
  local copies, waits for them, and re-layouts: 10 us -> 2.88 us
    dot_general x4 -> x0, matrix products: 110 us -> none  [advance(): jnp.dot(sens_part, weights_tile, preferred_element_type=jnp.float32)]
    psum x1 -> x0, blocking collectives: 79.2 us -> none  [per_device(): pulled_low = lax.psum(partial_pull, 'node').astype(jnp.bfloat16)]
    reduce_scatter x0 -> x1, waiting for transfers between devices: none -> 68.9 us  [per_device(): lax.psum_scatter(partial_pull, 'node', scatter_dimension=1, tiled=True)]
    pallas_call x0 -> x1, Pallas kernels: none -> 63.4 us  [pull_part(): pl.pallas_call(functools.partial(pull_kernel, rows, span, block), out_sha...]
    all_gather x0 -> x1, waiting for transfers between devices: none -> 38.4 us  [per_device(): lax.all_gather(pulled.astype(jnp.bfloat16), 'node', axis=1, tiled=True)]
    slice x8 -> x0, local copies, waits for them, and re-layouts: 8.35 us -> none  [kernel_tile(): delta_x = node_part[0][:, None] - ctrl_xyz[0][None, :]]
  transfers between devices with their start and end apart: 1 -> 3, of which waited for: 1 -> 3; matrix products, arithmetic and copies ran while one was open for 0% -> 0% of each run, Pallas kernels for 0% -> 0%
where the time goes in v1:
time: 211 us
  waiting for transfers between devices  120 us (57%)
  Pallas kernels  63.4 us (30%)
  between operations  13.1 us (6%)
  matrix products  9.79 us (5%)
  local copies, waits for them, and re-layouts  2.88 us (1%)
    reduce_scatter x1, waiting for transfers between devices, per_device(): lax.psum_scatter(partial_pull, 'node', scatter_dimension=1, tiled=True)  68.9 us
    pallas_call x1, Pallas kernels, pull_part(): pl.pallas_call(functools.partial(pull_kernel, rows, span, block), out_sha...  63.4 us
    all_gather x1, waiting for transfers between devices, per_device(): lax.all_gather(pulled.astype(jnp.bfloat16), 'node', axis=1, tiled=True)  38.4 us
    reduce_scatter x1, waiting for transfers between devices, per_device(): return lax.psum_scatter(product, 'ctrl', scatter_dimension=1, tiled=True)  12.4 us
    dot_general x1, matrix products, per_device(): product = jnp.dot(pulled_low, inverse, preferred_element_type=jnp.float32)  9.79 us
  transfers between devices with their start and end apart: 3, of which 3 were waited for; matrix products, arithmetic and copies ran while one was open for 0% of the time, Pallas kernels for 0%

profile of v1, /device:TPU:0, one launch (start us, length us, event | category | flops | bytes accessed | tf_op | source)
XLA Modules:
  0.0 210.6 jit_solution(17194575075768705773)
XLA Ops:
  6.5 0.0 reduce-scatter.3.cloned.1.call-start
  6.5 0.0 copy-start
  6.5 1.1 copy-done
  7.7 0.0 copy-start.1
  7.7 0.9 copy-done.1
  8.6 0.0 copy-start.2
  8.6 0.8 copy-done.2
  9.4 63.4 %shard_map.46 = f32[96,8192]{1,0:T(8,128)} custom-call(bf16[96,4096]{1,0:T(8,128)(2,1)S(1)} %copy-done, f32[3,4096]{1,0:T(4,128)S(1)} %copy-done.2, f32[3,8192]{1,0:T(4,128)S(1)} %copy-done.1), custom_call_target="tpu_custom_call" | custom-call | tf_op jit(solution)/shard_map/pallas_call | solution.py:87
  72.9 0.0 reduce-scatter.3.cloned.1.call-update
  72.9 0.0 all-gather.2.cloned.1.call-start
  72.9 68.9 %reduce-scatter.3.cloned.1.call-done = f32[96,512]{1,0:T(8,128)} async-done(((f32[96,8192]{1,0:T(8,128)}), f32[96,512]{1,0:T(8,128)}) %reduce-scatter.3.cloned.1.call-update) | async-done | bytes 196624 | tf_op jit(solution)/shard_map/reduce_scatter | solution.py:105
  141.8 1.6 convert_element_type.3
  143.4 0.0 all-gather.2.cloned.1.call-update
  143.4 0.0 reduce-scatter.5.cloned.1.call-start
  143.5 38.4 %all-gather.2.cloned.1.call-done = bf16[96,8192]{1,0:T(8,128)(2,1)} async-done(((bf16[96,512]{1,0:T(8,128)(2,1)}), bf16[96,8192]{1,0:T(8,128)(2,1)}) %all-gather.2.cloned.1.call-update) | async-done | bytes 1572880 | tf_op jit(solution)/shard_map/all_gather | solution.py:106
  181.9 9.8 %fusion = f32[96,1024]{1,0:T(8,128)} fusion(bf16[96,8192]{1,0:T(8,128)(2,1)} %all-gather.2.cloned.1.call-done, bf16[8192,1024]{1,0:T(8,128)(2,1)} %param.7), kind=kOutput, calls=%fused_computation | convolution fusion | flops 1610612736 | bytes 18743296 | tf_op jit(solution)/shard_map/dot_general | solution.py:107
  191.7 0.0 reduce-scatter.5.cloned.1.call-update
  191.7 12.4 %reduce-scatter.5.cloned.1.call-done = f32[96,512]{1,0:T(8,128)} async-done(((f32[96,1024]{1,0:T(8,128)}), f32[96,512]{1,0:T(8,128)}) %reduce-scatter.5.cloned.1.call-update) | async-done | bytes 196624 | tf_op jit(solution)/shard_map/reduce_scatter | solution.py:108
Async XLA Ops:
  6.5 135.3 %reduce-scatter.3.cloned.1.call-start = ((), (), s32[]{:S(2)}) async-start(), calls=%async_computation.2 | async-start | bytes 3342336 | tf_op jit(solution)/shard_map/reduce_scatter | solution.py:105
  6.5 1.1 copy-start
  7.7 0.9 copy-start.1
  8.6 0.8 copy-start.2
  72.9 109.0 %all-gather.2.cloned.1.call-start = ((), (), s32[]{:S(2)}) async-start(), calls=%async_computation.3 | async-start | bytes 1671168 | tf_op jit(solution)/shard_map/all_gather | solution.py:106
  143.4 60.6 %reduce-scatter.5.cloned.1.call-start = ((), (), s32[]{:S(2)}) async-start(), calls=%async_computation.4 | async-start | bytes 589824 | tf_op jit(solution)/shard_map/reduce_scatter | solution.py:108
Sparse Core Ops, SparseCore 0:
  73.0 68.7 reduce-scatter.2
  144.0 37.8 all-gather.1
  191.8 12.2 reduce-scatter.4

commit v2 on v1

v2 whole, which is shorter than its diff:
```python
import functools

import jax
import jax.numpy as jnp
from jax import lax
from jax.experimental import pallas as pl
from jax.experimental.pallas import tpu as pltpu
from jax.sharding import PartitionSpec as P

support_radius = 0.12
feature_rows = 32
max_chunks = 8


def split_three(value):
    high = value.astype(jnp.bfloat16).astype(jnp.float32)
    rest = value - high
    middle = rest.astype(jnp.bfloat16).astype(jnp.float32)
    return high, middle, rest - middle


def feature_pair(xyz, is_node):
    ones = jnp.ones_like(xyz[0:1])
    rows = []
    scaled = (xyz - 0.5) * (4.0 / support_radius)
    for axis in range(3):
        high, middle, low = split_three(scaled[axis : axis + 1])
        if is_node:
            rows += [high, high, middle, middle, high, low]
        else:
            rows += [-2.0 * part for part in (high, middle, high, middle, low, high)]
    square = scaled * scaled
    total = square[0:1] + square[1:2] + square[2:3]
    parts = list(split_three(total))
    rows += parts + [ones] * 3 if is_node else [ones] * 3 + parts
    rows += [jnp.zeros_like(ones)] * (feature_rows - len(rows))
    return rows


def fill_features(wide_ref, xyz_ref, is_node):
    for index, row in enumerate(feature_pair(xyz_ref[...], is_node)):
        wide_ref[pl.ds(index, 1), :] = row


def weights_of(square):
    square = jnp.maximum(square, 1e-12)
    remain = jnp.maximum(4.0 - square * lax.rsqrt(square), 0.0)
    twice = remain * remain
    return ((twice * twice) * (5.0 - remain)).astype(jnp.bfloat16)


def level_sizes(count):
    sizes = []
    while count % 2 == 0 and len(sizes) < 2:
        sizes.append(2)
        count //= 2
    return sizes + [count] if count > 1 else sizes


def fused_kernel(
    sizes, chunks, rows, span, block,
    sens_ref, node_ref, ctrl_ref, inverse_ref, out_ref,
    node_wide, ctrl_wide, node_feat, ctrl_feat, sens_t,
    inverse_here, inverse_sem, gathered, product, product_t, final, final_send, final_recv, *levels,
):
    nodes, ctrls = node_ref.shape[1], ctrl_ref.shape[1]
    depth = len(sizes)
    chunk = ctrls // chunks
    me = lax.axis_index("node")
    my_ctrl = lax.axis_index("ctrl")
    ctrl_count = final.shape[0] + 1
    own, sent, landed, rs_send, rs_recv, ag_send, ag_recv = [levels[i * depth : (i + 1) * depth] for i in range(7)]

    strides, lengths, coords, offsets = [], [chunk], [], [jnp.int32(0)]
    stride = 1
    for size in sizes:
        coord = lax.rem(lax.div(me, stride), size)
        strides.append(stride)
        lengths.append(lengths[-1] // size)
        coords.append(coord)
        offsets.append(offsets[-1] + coord * lengths[-1])
        stride *= size

    def peer_at(level, coord):
        return me + (coord - coords[level]) * strides[level]

    def around(level, turn):
        return lax.rem(coords[level] + turn + sizes[level], sizes[level])

    barrier = pltpu.get_barrier_semaphore()
    for level, size in enumerate(sizes):
        for turn in range(1, size):
            pl.semaphore_signal(barrier, inc=1, device_id={"node": peer_at(level, around(level, turn))}, device_id_type=pl.DeviceIdType.MESH)
    for turn in range(1, ctrl_count):
        other = lax.rem(my_ctrl + turn, ctrl_count)
        pl.semaphore_signal(barrier, inc=1, device_id={"ctrl": other}, device_id_type=pl.DeviceIdType.MESH)

    def inverse_copy(number):
        part = pl.ds(pl.multiple_of(number * chunk, chunk), chunk)
        return pltpu.make_async_copy(inverse_ref.at[part, :], inverse_here.at[part, :], inverse_sem.at[number])

    for number in range(chunks):
        inverse_copy(number).start()

    fill_features(node_wide, node_ref, True)
    fill_features(ctrl_wide, ctrl_ref, False)
    node_feat[...] = node_wide[...].astype(jnp.bfloat16)

    @pl.loop(0, nodes // block)
    def _(step):
        here = pl.ds(pl.multiple_of(step * block, block), block)
        sens_t[here, :] = sens_ref[:, here].astype(jnp.float32).T.astype(jnp.bfloat16)

    @pl.loop(0, ctrls // block)
    def _(step):
        here = pl.ds(pl.multiple_of(step * block, block), block)
        ctrl_feat[here, :] = ctrl_wide[:, here].T.astype(jnp.bfloat16)

    product[...] = jnp.zeros_like(product)
    pl.semaphore_wait(barrier, sum(size - 1 for size in sizes) + ctrl_count - 1)

    def scatter_copy(level, number, turn):
        coord = around(level, turn)
        length = lengths[level + 1]
        part = pl.ds(pl.multiple_of(coord * length, length), length)
        return pltpu.make_async_remote_copy(
            src_ref=sent[level].at[number, part, :],
            dst_ref=landed[level].at[number, turn - 1],
            send_sem=rs_send[level].at[number, turn - 1],
            recv_sem=rs_recv[level].at[number, turn - 1],
            device_id={"node": peer_at(level, coord)},
            device_id_type=pl.DeviceIdType.MESH,
        )

    def gather_copy(level, number, turn, arriving):
        length = lengths[level + 1]
        coord = around(level, -turn) if arriving else coords[level]
        start = offsets[level] + coord * length
        part = pl.ds(pl.multiple_of(start, length), length)
        return pltpu.make_async_remote_copy(
            src_ref=gathered.at[number, part, :],
            dst_ref=gathered.at[number, part, :],
            send_sem=ag_send[level].at[number, turn - 1],
            recv_sem=ag_recv[level].at[number, turn - 1],
            device_id={"node": peer_at(level, around(level, turn))},
            device_id_type=pl.DeviceIdType.MESH,
        )

    def start_scatter(level, number):
        for turn in range(1, sizes[level]):
            scatter_copy(level, number, turn).start()

    def start_gather(level, number):
        for turn in range(1, sizes[level]):
            gather_copy(level, number, turn, False).start()

    def compute(number):
        @pl.loop(0, chunk // rows)
        def _(step):
            there = pl.ds(pl.multiple_of(step * rows, rows), rows)
            left = ctrl_feat[pl.ds(pl.multiple_of(number * chunk + step * rows, rows), rows), :]

            def advance(index, total):
                for part in range(span // block):
                    offset = pl.multiple_of(index * span + part * block, block)
                    square = jnp.dot(left, node_feat[:, pl.ds(offset, block)], preferred_element_type=jnp.float32)
                    total = total + jnp.dot(weights_of(square), sens_t[pl.ds(offset, block), :], preferred_element_type=jnp.float32)
                return total

            own[0][number, there, :] = lax.fori_loop(0, nodes // span, advance, jnp.zeros((rows, sens_t.shape[1]), jnp.float32))

        start_scatter(0, number)

    def scatter_stage(level, number):
        length = lengths[level + 1]
        total = own[level][number, pl.ds(pl.multiple_of(coords[level] * length, length), length), :]
        for turn in range(1, sizes[level]):
            scatter_copy(level, number, turn).wait_recv()
            total = total + landed[level][number, turn - 1].astype(jnp.float32)
        if level + 1 < depth:
            own[level + 1][number] = total
            sent[level + 1][number] = total.astype(jnp.bfloat16)
            start_scatter(level + 1, number)
        else:
            part = pl.ds(pl.multiple_of(offsets[depth], length), length)
            gathered[number, part, :] = (total * (1.0 / 256.0)).astype(jnp.bfloat16)
            start_gather(level, number)

    def gather_stage(level, number):
        for turn in range(1, sizes[level]):
            gather_copy(level, number, turn, True).wait_recv()
        if level > 0:
            start_gather(level - 1, number)
        else:
            inverse_copy(number).wait()
            left = gathered[number].astype(jnp.float32).T.astype(jnp.bfloat16)
            part = pl.ds(pl.multiple_of(number * chunk, chunk), chunk)
            product[...] += jnp.dot(left, inverse_here[part, :], preferred_element_type=jnp.float32)

    stages = [compute]
    stages += [functools.partial(scatter_stage, level) for level in range(depth)]
    stages += [functools.partial(gather_stage, level) for level in reversed(range(depth))]

    @pl.loop(0, chunks + len(stages) - 1)
    def _(slot):
        for lag, stage in enumerate(stages):
            number = slot - lag

            @pl.when((number >= 0) & (number < chunks))
            def _():
                stage(number)

    width = final.shape[1]
    product_t[...] = product[...].T

    def final_copy(turn):
        other = lax.rem(my_ctrl + turn, ctrl_count)
        return pltpu.make_async_remote_copy(
            src_ref=product_t.at[pl.ds(pl.multiple_of(other * width, width), width), :],
            dst_ref=final.at[turn - 1],
            send_sem=final_send.at[turn - 1],
            recv_sem=final_recv.at[turn - 1],
            device_id={"ctrl": other},
            device_id_type=pl.DeviceIdType.MESH,
        )

    for turn in range(1, ctrl_count):
        final_copy(turn).start()

    @pl.loop(0, chunks)
    def _(number):
        for level, size in enumerate(sizes):
            for turn in range(1, size):
                scatter_copy(level, number, turn).wait_send()
                gather_copy(level, number, turn, False).wait_send()

    total = product_t[pl.ds(pl.multiple_of(my_ctrl * width, width), width), :]
    for turn in range(1, ctrl_count):
        final_copy(turn).wait_recv()
        total = total + final[turn - 1]
    out_ref[...] = total.T
    for turn in range(1, ctrl_count):
        final_copy(turn).wait_send()


def per_device(node_count, ctrl_count, sensitivity, node_xyz, ctrl_xyz, inverse):
    objs, nodes = sensitivity.shape
    ctrls, columns = inverse.shape
    sizes = level_sizes(node_count)
    chunks = max(1, min(max_chunks, ctrls // (16 * node_count)))
    chunk = ctrls // chunks
    rows, span, block = min(512, chunk), min(2048, nodes), min(256, nodes)
    lengths = [chunk]
    for size in sizes:
        lengths.append(lengths[-1] // size)
    depth = len(sizes)
    own = [pltpu.VMEM((chunks, lengths[level], objs), jnp.float32) for level in range(depth)]
    sent_types = [jnp.float32] + [jnp.bfloat16] * (depth - 1)
    sent = [pltpu.VMEM((chunks, lengths[level], objs), jnp.bfloat16) for level in range(1, depth)]
    landed = [pltpu.VMEM((chunks, sizes[level] - 1, lengths[level + 1], objs), sent_types[level]) for level in range(depth)]
    sems = [pltpu.SemaphoreType.DMA((chunks, size - 1)) for size in sizes]

    def kernel(*refs):
        first = len(refs) - (3 * depth - 1 + 4 * depth)
        levels = list(refs[first:])
        levels.insert(depth, levels[0])
        fused_kernel(sizes, chunks, rows, span, block, *refs[:first], *levels)

    width = columns // ctrl_count
    return pl.pallas_call(
        kernel,
        out_shape=jax.ShapeDtypeStruct((objs, width), jnp.float32),
        in_specs=[pl.BlockSpec(memory_space=pltpu.VMEM)] * 3 + [pl.BlockSpec(memory_space=pl.ANY)],
        out_specs=pl.BlockSpec(memory_space=pltpu.VMEM),
        scratch_shapes=[
            pltpu.VMEM((feature_rows, nodes), jnp.float32),
            pltpu.VMEM((feature_rows, ctrls), jnp.float32),
            pltpu.VMEM((feature_rows, nodes), jnp.bfloat16),
            pltpu.VMEM((ctrls, feature_rows), jnp.bfloat16),
            pltpu.VMEM((nodes, objs), jnp.bfloat16),
            pltpu.VMEM((ctrls, columns), jnp.bfloat16),
            pltpu.SemaphoreType.DMA((chunks,)),
            pltpu.VMEM((chunks, chunk, objs), jnp.bfloat16),
            pltpu.VMEM((objs, columns), jnp.float32),
            pltpu.VMEM((columns, objs), jnp.float32),
            pltpu.VMEM((ctrl_count - 1, width, objs), jnp.float32),
            pltpu.SemaphoreType.DMA((ctrl_count - 1,)),
            pltpu.SemaphoreType.DMA((ctrl_count - 1,)),
        ]
        + own + sent + landed + sems * 4,
        compiler_params=pltpu.CompilerParams(
            vmem_limit_bytes=56 * 2**20, collective_id=0, has_side_effects=True
        ),
    )(sensitivity, node_xyz, ctrl_xyz, inverse)


def solution(mesh):
    in_specs = (P(None, "node"), P(None, "node"), P(None, "ctrl"), P("ctrl", "node"))
    out_specs = P(None, ("node", "ctrl"))
    run = functools.partial(per_device, mesh.shape["node"], mesh.shape["ctrl"])
    return jax.shard_map(run, mesh=mesh, in_specs=in_specs, out_specs=out_specs, check_vma=False)
```

time: 211 us -> 96.3 us (0.46)
  waiting for transfers between devices: 120 us -> 0 us
  Pallas kernels: 63.4 us -> 94.5 us
  between operations: 13.1 us -> 0.01 us
  matrix products: 9.79 us -> 0 us
    reduce_scatter x2 -> x0, waiting for transfers between devices: 81.3 us -> none  [the longest x1 68.9 us: per_device(): lax.psum_scatter(partial_pull, 'node', scatter_dimension=1, tiled=True)]
    all_gather x1 -> x0, waiting for transfers between devices: 38.4 us -> none  [per_device(): lax.all_gather(pulled.astype(jnp.bfloat16), 'node', axis=1, tiled=True)]
    pallas_call x1, Pallas kernels: 63.4 us -> 94.5 us  [per_device(): pl.pallas_call(kernel, out_shape=jax.ShapeDtypeStruct((objs, width), jnp....]
    dot_general x1 -> x0, matrix products: 9.79 us -> none  [per_device(): product = jnp.dot(pulled_low, inverse, preferred_element_type=jnp.float32)]
  transfers between devices with their start and end apart: 3 -> 0, of which waited for: 3 -> 0; matrix products, arithmetic and copies ran while one was open for 0% -> 0% of each run, Pallas kernels for 0% -> 0%
where the time goes in v2:
time: 96.3 us; the launch traced here: 96.2 us
  Pallas kernels  94.5 us (98%)
  local copies, waits for them, and re-layouts  1.62 us (2%)
    pallas_call x1, Pallas kernels, per_device(): pl.pallas_call(kernel, out_shape=jax.ShapeDtypeStruct((objs, width), jnp....  94.5 us

profile of v2, /device:TPU:0, one launch (start us, length us, event | category | flops | bytes accessed | tf_op | source)
XLA Modules:
  0.0 96.2 jit_solution(15621660402280516131)
XLA Ops:
  0.0 94.5 %shard_map.46 = f32[96,512]{1,0:T(8,128)} custom-call(bf16[96,4096]{1,0:T(8,128)(2,1)} %refs_0_.1, f32[3,4096]{1,0:T(4,128)} %refs_1_.1, f32[3,8192]{1,0:T(4,128)} %refs_2_.1, bf16[8192,1024]{1,0:T(8,128)(2,1)} %refs_3_.1), custom_call_target="tpu_custom_call" | custom-call | tf_op jit(solution)/shard_map/pallas_call | solution.py:270
  94.5 1.6 %copy.6 = f32[96,512]{1,0:T(8,128)} copy(f32[96,512]{1,0:T(8,128)} %shard_map.46) | data formatting | bytes 393216

commit v3 on v2

--- a/solution.py
+++ b/solution.py
@@ -50,17 +50,13 @@
 
 
 def level_sizes(count):
-    sizes = []
-    while count % 2 == 0 and len(sizes) < 2:
-        sizes.append(2)
-        count //= 2
-    return sizes + [count] if count > 1 else sizes
+    return [2, count // 2] if count % 2 == 0 and count > 2 else [count]
 
 
 def fused_kernel(
     sizes, chunks, rows, span, block,
     sens_ref, node_ref, ctrl_ref, inverse_ref, out_ref,
-    node_wide, ctrl_wide, node_feat, ctrl_feat, sens_t,
+    node_wide, ctrl_wide, node_feat, ctrl_feat,
     inverse_here, inverse_sem, gathered, product, product_t, final, final_send, final_recv, *levels,
 ):
     nodes, ctrls = node_ref.shape[1], ctrl_ref.shape[1]
@@ -104,17 +100,12 @@
 
     fill_features(node_wide, node_ref, True)
     fill_features(ctrl_wide, ctrl_ref, False)
-    node_feat[...] = node_wide[...].astype(jnp.bfloat16)
+    ctrl_feat[...] = ctrl_wide[...].astype(jnp.bfloat16)
 
     @pl.loop(0, nodes // block)
     def _(step):
         here = pl.ds(pl.multiple_of(step * block, block), block)
-        sens_t[here, :] = sens_ref[:, here].astype(jnp.float32).T.astype(jnp.bfloat16)
-
-    @pl.loop(0, ctrls // block)
-    def _(step):
-        here = pl.ds(pl.multiple_of(step * block, block), block)
-        ctrl_feat[here, :] = ctrl_wide[:, here].T.astype(jnp.bfloat16)
+        node_feat[here, :] = node_wide[:, here].T.astype(jnp.bfloat16)
 
     product[...] = jnp.zeros_like(product)
     pl.semaphore_wait(barrier, sum(size - 1 for size in sizes) + ctrl_count - 1)
@@ -158,16 +149,16 @@
         @pl.loop(0, chunk // rows)
         def _(step):
             there = pl.ds(pl.multiple_of(step * rows, rows), rows)
-            left = ctrl_feat[pl.ds(pl.multiple_of(number * chunk + step * rows, rows), rows), :]
+            right = ctrl_feat[:, pl.ds(pl.multiple_of(number * chunk + step * rows, rows), rows)]
 
             def advance(index, total):
                 for part in range(span // block):
                     offset = pl.multiple_of(index * span + part * block, block)
-                    square = jnp.dot(left, node_feat[:, pl.ds(offset, block)], preferred_element_type=jnp.float32)
-                    total = total + jnp.dot(weights_of(square), sens_t[pl.ds(offset, block), :], preferred_element_type=jnp.float32)
+                    square = jnp.dot(node_feat[pl.ds(offset, block), :], right, preferred_element_type=jnp.float32)
+                    total = total + jnp.dot(sens_ref[:, pl.ds(offset, block)], weights_of(square), preferred_element_type=jnp.float32)
                 return total
 
-            own[0][number, there, :] = lax.fori_loop(0, nodes // span, advance, jnp.zeros((rows, sens_t.shape[1]), jnp.float32))
+            own[0][number, there, :] = lax.fori_loop(0, nodes // span, advance, jnp.zeros((sens_ref.shape[0], rows), jnp.float32)).T
 
         start_scatter(0, number)
 
@@ -275,9 +266,8 @@
         scratch_shapes=[
             pltpu.VMEM((feature_rows, nodes), jnp.float32),
             pltpu.VMEM((feature_rows, ctrls), jnp.float32),
-            pltpu.VMEM((feature_rows, nodes), jnp.bfloat16),
-            pltpu.VMEM((ctrls, feature_rows), jnp.bfloat16),
-            pltpu.VMEM((nodes, objs), jnp.bfloat16),
+            pltpu.VMEM((nodes, feature_rows), jnp.bfloat16),
+            pltpu.VMEM((feature_rows, ctrls), jnp.bfloat16),
             pltpu.VMEM((ctrls, columns), jnp.bfloat16),
             pltpu.SemaphoreType.DMA((chunks,)),
             pltpu.VMEM((chunks, chunk, objs), jnp.bfloat16),

time: 96.3 us -> 134 us (1.39)
  Pallas kernels: 94.5 us -> 132 us
    pallas_call x1, Pallas kernels: 94.5 us -> 132 us  [per_device(): pl.pallas_call(kernel, out_shape=jax.ShapeDtypeStruct((objs, width), jnp....]
where the time goes in v3:
time: 134 us
  Pallas kernels  132 us (99%)
  local copies, waits for them, and re-layouts  1.62 us (1%)
    pallas_call x1, Pallas kernels, per_device(): pl.pallas_call(kernel, out_shape=jax.ShapeDtypeStruct((objs, width), jnp....  132 us

profile of v3, /device:TPU:0, one launch (start us, length us, event | category | flops | bytes accessed | tf_op | source)
XLA Modules:
  0.0 134.1 jit_solution(9865702660758122466)
XLA Ops:
  0.0 132.5 %shard_map.46 = f32[96,512]{1,0:T(8,128)} custom-call(bf16[96,4096]{1,0:T(8,128)(2,1)} %refs_0_.1, f32[3,4096]{1,0:T(4,128)} %refs_1_.1, f32[3,8192]{1,0:T(4,128)} %refs_2_.1, bf16[8192,1024]{1,0:T(8,128)(2,1)} %refs_3_.1), custom_call_target="tpu_custom_call" | custom-call | tf_op jit(solution)/shard_map/pallas_call | solution.py:261
  132.5 1.6 %copy.6 = f32[96,512]{1,0:T(8,128)} copy(f32[96,512]{1,0:T(8,128)} %shard_map.46) | data formatting | bytes 393216

commit v4 on v2

--- a/solution.py
+++ b/solution.py
@@ -50,18 +50,14 @@
 
 
 def level_sizes(count):
-    sizes = []
-    while count % 2 == 0 and len(sizes) < 2:
-        sizes.append(2)
-        count //= 2
-    return sizes + [count] if count > 1 else sizes
+    return [2, count // 2] if count % 2 == 0 and count > 2 else [count]
 
 
 def fused_kernel(
     sizes, chunks, rows, span, block,
     sens_ref, node_ref, ctrl_ref, inverse_ref, out_ref,
     node_wide, ctrl_wide, node_feat, ctrl_feat, sens_t,
-    inverse_here, inverse_sem, gathered, product, product_t, final, final_send, final_recv, *levels,
+    inverse_here, inverse_sem, gathered, product, product_t, product_low, final, final_send, final_recv, *levels,
 ):
     nodes, ctrls = node_ref.shape[1], ctrl_ref.shape[1]
     depth = len(sizes)
@@ -212,11 +208,12 @@
 
     width = final.shape[1]
     product_t[...] = product[...].T
+    product_low[...] = product_t[...].astype(jnp.bfloat16)
 
     def final_copy(turn):
         other = lax.rem(my_ctrl + turn, ctrl_count)
         return pltpu.make_async_remote_copy(
-            src_ref=product_t.at[pl.ds(pl.multiple_of(other * width, width), width), :],
+            src_ref=product_low.at[pl.ds(pl.multiple_of(other * width, width), width), :],
             dst_ref=final.at[turn - 1],
             send_sem=final_send.at[turn - 1],
             recv_sem=final_recv.at[turn - 1],
@@ -237,7 +234,7 @@
     total = product_t[pl.ds(pl.multiple_of(my_ctrl * width, width), width), :]
     for turn in range(1, ctrl_count):
         final_copy(turn).wait_recv()
-        total = total + final[turn - 1]
+        total = total + final[turn - 1].astype(jnp.float32)
     out_ref[...] = total.T
     for turn in range(1, ctrl_count):
         final_copy(turn).wait_send()
@@ -249,7 +246,7 @@
     sizes = level_sizes(node_count)
     chunks = max(1, min(max_chunks, ctrls // (16 * node_count)))
     chunk = ctrls // chunks
-    rows, span, block = min(512, chunk), min(2048, nodes), min(256, nodes)
+    rows, span, block = min(1024, chunk), min(2048, nodes), min(256, nodes)
     lengths = [chunk]
     for size in sizes:
         lengths.append(lengths[-1] // size)
@@ -283,7 +280,8 @@
             pltpu.VMEM((chunks, chunk, objs), jnp.bfloat16),
             pltpu.VMEM((objs, columns), jnp.float32),
             pltpu.VMEM((columns, objs), jnp.float32),
-            pltpu.VMEM((ctrl_count - 1, width, objs), jnp.float32),
+            pltpu.VMEM((columns, objs), jnp.bfloat16),
+            pltpu.VMEM((ctrl_count - 1, width, objs), jnp.bfloat16),
             pltpu.SemaphoreType.DMA((ctrl_count - 1,)),
             pltpu.SemaphoreType.DMA((ctrl_count - 1,)),
         ]

time: 96.3 us -> 93 us (0.966)
  Pallas kernels: 94.5 us -> 91.3 us
    pallas_call x1, Pallas kernels: 94.5 us -> 91.3 us  [per_device(): pl.pallas_call(kernel, out_shape=jax.ShapeDtypeStruct((objs, width), jnp....]
where the time goes in v4:
time: 93 us; the launch traced here: 92.9 us
  Pallas kernels  91.3 us (98%)
  local copies, waits for them, and re-layouts  1.62 us (2%)
    pallas_call x1, Pallas kernels, per_device(): pl.pallas_call(kernel, out_shape=jax.ShapeDtypeStruct((objs, width), jnp....  91.3 us

profile of v4, /device:TPU:0, one launch (start us, length us, event | category | flops | bytes accessed | tf_op | source)
XLA Modules:
  0.0 92.9 jit_solution(17366348959988229914)
XLA Ops:
  0.0 91.3 %shard_map.46 = f32[96,512]{1,0:T(8,128)} custom-call(bf16[96,4096]{1,0:T(8,128)(2,1)} %refs_0_.1, f32[3,4096]{1,0:T(4,128)} %refs_1_.1, f32[3,8192]{1,0:T(4,128)} %refs_2_.1, bf16[8192,1024]{1,0:T(8,128)(2,1)} %refs_3_.1), custom_call_target="tpu_custom_call" | custom-call | tf_op jit(solution)/shard_map/pallas_call | solution.py:267
  91.3 1.6 %copy.6 = f32[96,512]{1,0:T(8,128)} copy(f32[96,512]{1,0:T(8,128)} %shard_map.46) | data formatting | bytes 393216

commit v5 on v4

--- a/solution.py
+++ b/solution.py
@@ -10,6 +10,7 @@
 support_radius = 0.12
 feature_rows = 32
 max_chunks = 8
+half_per_log_two = 0.7213475204444817
 
 
 def split_three(value):
@@ -44,7 +45,7 @@
 
 def weights_of(square):
     square = jnp.maximum(square, 1e-12)
-    remain = jnp.maximum(4.0 - square * lax.rsqrt(square), 0.0)
+    remain = jnp.maximum(4.0 - jnp.exp2(jnp.log(square) * half_per_log_two), 0.0)
     twice = remain * remain
     return ((twice * twice) * (5.0 - remain)).astype(jnp.bfloat16)
 

time: 93 us -> 97.9 us (1.053)
  Pallas kernels: 91.3 us -> 96.1 us
    pallas_call x1, Pallas kernels: 91.3 us -> 96.1 us  [per_device(): pl.pallas_call(kernel, out_shape=jax.ShapeDtypeStruct((objs, width), jnp....]
where the time goes in v5:
time: 97.9 us; the launch traced here: 97.7 us
  Pallas kernels  96.1 us (98%)
  local copies, waits for them, and re-layouts  1.62 us (2%)
    pallas_call x1, Pallas kernels, per_device(): pl.pallas_call(kernel, out_shape=jax.ShapeDtypeStruct((objs, width), jnp....  96.1 us

profile of v5, /device:TPU:0, one launch (start us, length us, event | category | flops | bytes accessed | tf_op | source)
XLA Modules:
  0.0 97.7 jit_solution(15028523100320665556)
XLA Ops:
  0.0 96.1 %shard_map.46 = f32[96,512]{1,0:T(8,128)} custom-call(bf16[96,4096]{1,0:T(8,128)(2,1)} %refs_0_.1, f32[3,4096]{1,0:T(4,128)} %refs_1_.1, f32[3,8192]{1,0:T(4,128)} %refs_2_.1, bf16[8192,1024]{1,0:T(8,128)(2,1)} %refs_3_.1), custom_call_target="tpu_custom_call" | custom-call | tf_op jit(solution)/shard_map/pallas_call | solution.py:268
  96.1 1.6 %copy.6 = f32[96,512]{1,0:T(8,128)} copy(f32[96,512]{1,0:T(8,128)} %shard_map.46) | data formatting | bytes 393216

commit v6 on v4

--- a/solution.py
+++ b/solution.py
@@ -10,6 +10,8 @@
 support_radius = 0.12
 feature_rows = 32
 max_chunks = 8
+ctrl_plain, node_plain = 24, 27
+lanes = 128
 
 
 def split_three(value):
@@ -33,6 +35,8 @@
     total = square[0:1] + square[1:2] + square[2:3]
     parts = list(split_three(total))
     rows += parts + [ones] * 3 if is_node else [ones] * 3 + parts
+    plain, zeros = [scaled[axis : axis + 1] for axis in range(3)], [jnp.zeros_like(ones)] * 3
+    rows += zeros + plain if is_node else plain + zeros
     rows += [jnp.zeros_like(ones)] * (feature_rows - len(rows))
     return rows
 
@@ -56,7 +60,7 @@
 def fused_kernel(
     sizes, chunks, rows, span, block,
     sens_ref, node_ref, ctrl_ref, inverse_ref, out_ref,
-    node_wide, ctrl_wide, node_feat, ctrl_feat, sens_t,
+    node_wide, ctrl_wide, node_feat, ctrl_feat, sens_t, ctrl_spread,
     inverse_here, inverse_sem, gathered, product, product_t, product_low, final, final_send, final_recv, *levels,
 ):
     nodes, ctrls = node_ref.shape[1], ctrl_ref.shape[1]
@@ -110,7 +114,10 @@
     @pl.loop(0, ctrls // block)
     def _(step):
         here = pl.ds(pl.multiple_of(step * block, block), block)
-        ctrl_feat[here, :] = ctrl_wide[:, here].T.astype(jnp.bfloat16)
+        turned = ctrl_wide[:, here].T
+        ctrl_feat[here, :] = turned.astype(jnp.bfloat16)
+        for axis in range(3):
+            ctrl_spread[axis, here, :] = jnp.broadcast_to(turned[:, ctrl_plain + axis : ctrl_plain + axis + 1], (block, lanes))
 
     product[...] = jnp.zeros_like(product)
     pl.semaphore_wait(barrier, sum(size - 1 for size in sizes) + ctrl_count - 1)
@@ -150,17 +157,29 @@
         for turn in range(1, sizes[level]):
             gather_copy(level, number, turn, False).start()
 
+    def plain_square(here, offset):
+        total = None
+        for axis in range(3):
+            node_row = node_wide[pl.ds(node_plain + axis, 1), pl.ds(pl.multiple_of(offset, lanes), lanes)]
+            delta = ctrl_spread[axis, here, :] - node_row
+            total = delta * delta if total is None else total + delta * delta
+        return total
+
     def compute(number):
         @pl.loop(0, chunk // rows)
         def _(step):
             there = pl.ds(pl.multiple_of(step * rows, rows), rows)
-            left = ctrl_feat[pl.ds(pl.multiple_of(number * chunk + step * rows, rows), rows), :]
+            here = pl.ds(pl.multiple_of(number * chunk + step * rows, rows), rows)
+            left = ctrl_feat[here, :]
 
             def advance(index, total):
                 for part in range(span // block):
                     offset = pl.multiple_of(index * span + part * block, block)
-                    square = jnp.dot(left, node_feat[:, pl.ds(offset, block)], preferred_element_type=jnp.float32)
-                    total = total + jnp.dot(weights_of(square), sens_t[pl.ds(offset, block), :], preferred_element_type=jnp.float32)
+                    if part % 3 == 1 and block % lanes == 0:
+                        weights = jnp.concatenate([weights_of(plain_square(here, offset + piece * lanes)) for piece in range(block // lanes)], axis=1)
+                    else:
+                        weights = weights_of(jnp.dot(left, node_feat[:, pl.ds(offset, block)], preferred_element_type=jnp.float32))
+                    total = total + jnp.dot(weights, sens_t[pl.ds(offset, block), :], preferred_element_type=jnp.float32)
                 return total
 
             own[0][number, there, :] = lax.fori_loop(0, nodes // span, advance, jnp.zeros((rows, sens_t.shape[1]), jnp.float32))
@@ -275,6 +294,7 @@
             pltpu.VMEM((feature_rows, nodes), jnp.bfloat16),
             pltpu.VMEM((ctrls, feature_rows), jnp.bfloat16),
             pltpu.VMEM((nodes, objs), jnp.bfloat16),
+            pltpu.VMEM((3, ctrls, lanes), jnp.float32),
             pltpu.VMEM((ctrls, columns), jnp.bfloat16),
             pltpu.SemaphoreType.DMA((chunks,)),
             pltpu.VMEM((chunks, chunk, objs), jnp.bfloat16),

time: 93 us -> 109 us (1.17)
  Pallas kernels: 91.3 us -> 107 us
    pallas_call x1, Pallas kernels: 91.3 us -> 107 us  [per_device(): pl.pallas_call(kernel, out_shape=jax.ShapeDtypeStruct((objs, width), jnp....]
where the time goes in v6:
time: 109 us
  Pallas kernels  107 us (98%)
  local copies, waits for them, and re-layouts  1.62 us (1%)
    pallas_call x1, Pallas kernels, per_device(): pl.pallas_call(kernel, out_shape=jax.ShapeDtypeStruct((objs, width), jnp....  107 us

profile of v6, /device:TPU:0, one launch (start us, length us, event | category | flops | bytes accessed | tf_op | source)
XLA Modules:
  0.0 109.1 jit_solution(18095020895155431202)
XLA Ops:
  0.0 107.5 %shard_map.46 = f32[96,512]{1,0:T(8,128)} custom-call(bf16[96,4096]{1,0:T(8,128)(2,1)} %refs_0_.1, f32[3,4096]{1,0:T(4,128)} %refs_1_.1, f32[3,8192]{1,0:T(4,128)} %refs_2_.1, bf16[8192,1024]{1,0:T(8,128)(2,1)} %refs_3_.1), custom_call_target="tpu_custom_call" | custom-call | tf_op jit(solution)/shard_map/pallas_call | solution.py:286
  107.5 1.6 %copy.6 = f32[96,512]{1,0:T(8,128)} copy(f32[96,512]{1,0:T(8,128)} %shard_map.46) | data formatting | bytes 393216
